TPU v7x, 128 devices: a whole 4x4x4 slice. The times are simulated.
128 devices in a mesh: feat: 64 (over y, x, z), batch: 2 (over core).
Axes of the slice: x: 4, y: 4, z: 4, core: 2. Of those that a mesh axis runs over, the one named last changes fastest.
Arguments:
- features: bfloat16 [1024, 131072], P('batch', 'feat'), may hold values from -6 to 6
- cotangent: bfloat16 [1024, 131072], P('batch', 'feat'), may hold values from -6 to 6
- u_rows: bfloat16 [131072, 1024], P('feat'), may hold values from -0.1875 to 0.1875
- v_rows: bfloat16 [131072, 1024], P('feat'), may hold values from -0.046875 to 0.046875
- bias: float32 [131072], P('feat'), may hold values from -6 to 6
Outputs:
- grad_input: bfloat16 [1024, 131072], P('batch', 'feat')
- grad_u: bfloat16 [131072, 1024], P('feat', 'batch')
- grad_v: bfloat16 [131072, 1024], P('feat', 'batch')
- grad_bias: float32 [131072], P('feat')
All inputs are finite; a program needn't handle non-finite values.
Results may differ from a plain program's by a relative error of at most 0.0065.
Values may be sent and summed in bfloat16 or wider, within the bound.
A program may use at most 128 MiB of HBM per device.

v0:
```python
import jax
import jax.numpy as jnp
from jax import lax
from jax.sharding import PartitionSpec as P


def shards(features, cotangent, u_rows, v_rows, bias):
    partial_codes = jnp.dot(features, v_rows, preferred_element_type=jnp.float32)
    codes = lax.psum(partial_codes, "feat").astype(jnp.bfloat16)
    lifted = lax.dot_general(
        codes, u_rows, (((1,), (1,)), ((), ())), preferred_element_type=jnp.float32
    )
    grad_out = cotangent.astype(jnp.float32)
    dlift = (grad_out * features.astype(jnp.float32)).astype(jnp.bfloat16)
    partial_dcodes = jnp.dot(dlift, u_rows, preferred_element_type=jnp.float32)
    dcodes = lax.psum(partial_dcodes, "feat").astype(jnp.bfloat16)
    back = lax.dot_general(
        dcodes, v_rows, (((1,), (1,)), ((), ())), preferred_element_type=jnp.float32
    )
    grad_input = (grad_out * (lifted + bias[None, :] + 1.0) + back).astype(jnp.bfloat16)
    local_u = lax.dot_general(
        dlift, codes, (((0,), (0,)), ((), ())), preferred_element_type=jnp.float32
    )
    local_v = lax.dot_general(
        features, dcodes, (((0,), (0,)), ((), ())), preferred_element_type=jnp.float32
    )
    summed_u, summed_v = (
        lax.psum_scatter(local_u, "batch", scatter_dimension=1, tiled=True),
        lax.psum_scatter(local_v, "batch", scatter_dimension=1, tiled=True),
    )
    grad_u = summed_u.astype(jnp.bfloat16)
    grad_v = summed_v.astype(jnp.bfloat16)
    grad_bias = lax.psum(jnp.sum(dlift.astype(jnp.float32), axis=0), "batch")
    return (grad_input, grad_u, grad_v, grad_bias)


def solution(mesh):
    in_specs = (P("batch", "feat"), P("batch", "feat"), P("feat", None), P("feat", None), P("feat"))
    out_specs = (P("batch", "feat"), P("feat", "batch"), P("feat", "batch"), P("feat"))
    return jax.shard_map(shards, mesh=mesh, in_specs=in_specs, out_specs=out_specs, check_vma=False)
```

profile of v0, /device:TPU:0, one launch (start us, length us, event | category | flops | bytes accessed | tf_op | source)
XLA Modules:
  0.0 472.9 jit_solution(1811469207193446780)
XLA Ops:
  7.2 0.0 copy-start
  7.2 0.0 reduce-scatter.5.cloned.1.call-start
  7.2 0.0 copy-start.2
  7.2 7.3 %fusion.10 = f32[512,1024]{1,0:T(8,128)} fusion(bf16[2048,1024]{1,0:T(8,128)(2,1)} %param.7, bf16[512,2048]{1,0:T(8,128)(2,1)} %param.6, bf16[512,2048]{1,0:T(8,128)(2,1)} %param.5), kind=kOutput, calls=%fused_computation.13 | convolution fusion | flops 2151677952 | bytes 10485760 | tf_op jit(solution)/shard_map/dot_general | solution.py:15
  14.5 0.0 copy-done
  14.5 0.0 copy-done.2
  14.5 3.7 fusion.12
  18.2 399.9 %all-reduce.2 = (bf16[512,1024]{1,0:T(8,128)(2,1)S(1)}, bf16[512,1024]{1,0:T(8,128)(2,1)}) all-reduce(f32[512,1024]{1,0:T(8,128)} %fusion.12, f32[512,1024]{1,0:T(8,128)} %fusion.10), channel_id=1, replica_groups=mesh['feat'=64,'batch'=2] {'feat'}, use_global_device_ids=true, to_apply=%region_0.0 | all-reduce | flops 1048576 | bytes 6291456 | tf_op jit(solution)/shard_map/psum | solution.py:9
  418.1 6.8 %convolution_bitcast_fusion = f32[2048,1024]{0,1:T(8,128)} fusion(bf16[512,2048]{1,0:T(8,128)(2,1)S(1)} %copy-done, bf16[512,1024]{1,0:T(8,128)(2,1)} %get-tuple-element.9), kind=kOutput, calls=%fused_computation.2 | convolution fusion | flops 2147483648 | bytes 11534336 | tf_op jit(solution)/shard_map/dot_general | solution.py:24
  424.9 0.0 reduce-scatter.5.cloned.1.call-update
  424.9 0.0 reduce-scatter.3.cloned.1.call-start
  424.9 8.8 %fusion.5 = f32[2048,1024]{1,0:T(8,128)} fusion(bf16[512,1024]{1,0:T(8,128)(2,1)S(1)} %get-tuple-element.8, bf16[512,2048]{1,0:T(8,128)(2,1)} %param.6, bf16[512,2048]{1,0:T(8,128)(2,1)S(1)} %copy-done), kind=kOutput, calls=%fused_computation.9 | convolution fusion | flops 2151677952 | bytes 13631488 | tf_op jit(solution)/shard_map/dot_general | solution.py:21
  433.7 0.0 reduce-scatter.3.cloned.1.call-update
  433.7 2.8 convert_reduce_fusion
  436.5 3.3 psum.23
  439.8 0.0 copy-start.1
  439.8 0.0 copy-start.3
  439.8 0.0 copy-start.4
  439.8 0.0 copy-start.5
  439.8 4.7 fusion.13
  444.5 0.0 copy-done.1
  444.5 0.0 copy-done.3
  444.5 0.0 copy-done.4
  444.6 0.0 copy-done.5
  444.6 3.9 fusion.1
  448.5 0.0 reduce-scatter.5.cloned.1.call-done
  448.5 2.5 convert_element_type.34
  451.0 2.5 copy.9
  453.5 8.8 %reduce-scatter.3.cloned.1.call-done = f32[2048,512]{1,0:T(8,128)} async-done(((f32[2048,1024]{1,0:T(8,128)}), f32[2048,512]{1,0:T(8,128)}) %reduce-scatter.3.cloned.1.call-update) | async-done | bytes 4194320 | tf_op jit(solution)/shard_map/reduce_scatter | solution.py:28
  462.3 3.8 convert_element_type.33
Async XLA Ops:
  7.2 7.3 %copy-start = (bf16[512,2048]{1,0:T(8,128)(2,1)S(1)}, bf16[512,2048]{1,0:T(8,128)(2,1)}, u32[]{:S(2)}) copy-start(bf16[512,2048]{1,0:T(8,128)(2,1)} %param.5) | copy-start | bytes 6291460
  7.2 441.3 %reduce-scatter.5.cloned.1.call-start = ((), (), s32[]{:S(2)}) async-start(), calls=%async_computation.3 | async-start | bytes 12582912 | tf_op jit(solution)/shard_map/reduce_scatter | solution.py:29
  7.2 7.3 %copy-start.2 = (bf16[2048,1024]{1,0:T(8,128)(2,1)S(1)}, bf16[2048,1024]{1,0:T(8,128)(2,1)}, u32[]{:S(2)}) copy-start(bf16[2048,1024]{1,0:T(8,128)(2,1)} %param.8) | copy-start | bytes 12582916
  424.9 37.4 %reduce-scatter.3.cloned.1.call-start = ((), (), s32[]{:S(2)}) async-start(), calls=%async_computation.2 | async-start | bytes 12582912 | tf_op jit(solution)/shard_map/reduce_scatter | solution.py:28
  439.8 4.7 copy-start.1
  439.8 4.7 %copy-start.3 = (bf16[2048,1024]{1,0:T(8,128)(2,1)S(1)}, bf16[2048,1024]{1,0:T(8,128)(2,1)}, u32[]{:S(2)}) copy-start(bf16[2048,1024]{1,0:T(8,128)(2,1)} %param.8) | copy-start | bytes 12582916
  439.8 4.7 %copy-start.4 = (bf16[512,1024]{1,0:T(8,128)(2,1)S(1)}, bf16[512,1024]{1,0:T(8,128)(2,1)}, u32[]{:S(2)}) copy-start(bf16[512,1024]{1,0:T(8,128)(2,1)} %get-tuple-element.9) | copy-start | bytes 3145732
  439.8 4.7 %copy-start.5 = (f32[2048]{0:T(1024)S(1)}, f32[2048]{0:T(1024)}, u32[]{:S(2)}) copy-start(f32[2048]{0:T(1024)} %param.9) | copy-start | bytes 24580
Sparse Core Ops, SparseCore 0:
  425.0 13.7 reduce-scatter.4
  441.3 20.9 reduce-scatter.2
where the time goes:
time: 474 us; the launch traced here: 473 us
  blocking collectives  403 us (85%)
  matrix products  35.2 us (7%)
  between operations  14.1 us (3%)
  other arithmetic  9.07 us (2%)
  waiting for transfers between devices  8.85 us (2%)
    psum x1, blocking collectives, shards(): codes = lax.psum(partial_codes, 'feat').astype(jnp.bfloat16)  400 us
  transfers between devices with their start and end apart: 2, of which 1 were waited for; matrix products, arithmetic and copies ran while one was open for 5% of the time, Pallas kernels for 0%

commit v1 on v0

v1 whole, which is shorter than its diff:
```python
import jax
import jax.numpy as jnp
from jax import lax
from jax.experimental import pallas as pl
from jax.experimental.pallas import tpu as pltpu
from jax.sharding import PartitionSpec as P

MESH = pl.DeviceIdType.MESH
F32, BF16 = jnp.float32, jnp.bfloat16
ROWS, COLS, RANK = 512, 2048, 1024
BLOCK = 256
TILES = 256
HALVINGS, DIMS = 4, 6
STAGES = DIMS + HALVINGS
SIZES = ((48, 48, 48, 48, 32, 32), (48, 48, 48, 32, 32, 48))
TURNS = (0, 3)
AXES = ((16, 0), (4, 0), (1, 0), (16, 1), (4, 1), (1, 1))


def partners(feat):
    bits, others = [], []
    for stride, kind in AXES:
        place = lax.rem(lax.div(feat, stride), 4)
        if kind == 0:
            bits.append(lax.rem(lax.div(place + 1, 2), 2))
            other = place + 1 - 2 * lax.rem(place, 2)
        else:
            bits.append(lax.div(place, 2))
            other = 3 - place
        others.append(feat + (other - place) * stride)
    return bits, others


class Sum:
    def __init__(self, index, bits, others, core, acc, out, got, mid, full, send_sem, recv_sem):
        self.index, self.bits, self.others, self.core = index, bits, others, core
        self.acc, self.out, self.got, self.mid, self.full = acc, out, got, mid, full
        self.send_sem, self.recv_sem = send_sem, recv_sem
        self.sizes = SIZES[index]
        self.starts = [sum(self.sizes[:part]) for part in range(6)]
        self.copies, self.region, self.past = {}, {}, {}
        offset, self.offset = 0, {}
        for stage in range(DIMS):
            for part in range(6):
                self.offset[stage, part] = offset
                offset += self.sizes[part] >> min(stage + 1, HALVINGS)
        offset, self.place = 0, {}
        for stage in range(HALVINGS, DIMS):
            for part in range(6):
                self.place[stage, part] = offset
                offset += self.sizes[part] >> HALVINGS

    def dim(self, part, stage):
        return (part + stage + TURNS[self.index]) % DIMS

    def start(self, part, stage, source, target):
        copy = pltpu.make_async_remote_copy(
            src_ref=source,
            dst_ref=target,
            send_sem=self.send_sem.at[stage, part],
            recv_sem=self.recv_sem.at[stage, part],
            device_id=(self.others[self.dim(part, stage if stage < DIMS else STAGES - 1 - stage)], self.core),
            device_id_type=MESH,
        )
        copy.start()
        self.copies[stage, part] = copy

    def send(self, part, stage):
        if stage == 0:
            self.region[part] = (self.starts[part], self.sizes[part])
        start, size = self.region[part]
        if stage < HALVINGS:
            half = size // 2
            bit = self.bits[self.dim(part, stage)]
            away = start + (1 - bit) * half
            self.past[part, stage] = start
            self.region[part] = (start + bit * half, half)
            self.start(part, stage, self.out.at[pl.ds(away, half)], self.got.at[pl.ds(self.offset[stage, part], half)])
        elif stage < DIMS:
            self.start(part, stage, self.mid.at[pl.ds(self.place[stage, part], size)], self.got.at[pl.ds(self.offset[stage, part], size)])
        else:
            where = self.full.at[pl.ds(start, size)]
            self.start(part, stage, where, where)

    def receive(self, part, stage):
        self.copies[stage, part].wait_recv()
        start, size = self.region[part]
        if stage < DIMS:
            here = pl.ds(start, size)
            value = self.acc[here] + self.got[pl.ds(self.offset[stage, part], size)].astype(F32)
            if stage == DIMS - 1:
                self.full[here] = value.astype(BF16)
            else:
                self.acc[here] = value
                if stage + 1 < HALVINGS:
                    self.out[here] = value.astype(BF16)
                else:
                    self.mid[pl.ds(self.place[stage + 1, part], size)] = value.astype(BF16)
        else:
            self.region[part] = (self.past[part, STAGES - 1 - stage], 2 * size)

    def step(self, stage):
        for part in range(6):
            self.receive(part, stage)
            if stage + 1 < STAGES:
                self.send(part, stage + 1)

    def finish(self):
        for copy in self.copies.values():
            copy.wait_send()


def kernel(
    f_hbm, c_hbm, u_hbm, v_hbm, b_ref, gi_hbm, gu_hbm, gv_hbm, gb_ref,
    f, c, u, v, d, acc_a, acc_b, out_a, out_b, got_a, got_b, mid_a, mid_b, full_a, full_b,
    ft, dt, base, codes, dcodes, half_a, half_b, twin_a, twin_b, gi, gu, gv, bias_own, bias_twin,
    load_sem, store_sem, send_a, recv_a, send_b, recv_b, twin_send, twin_recv,
):
    feat, core = lax.axis_index("feat"), lax.axis_index("batch")
    twin = (feat, 1 - core)
    bits, others = partners(feat)

    loads = [pltpu.make_async_copy(f_hbm, f, load_sem.at[0])]
    for j in range(4):
        cols = pl.ds(j * BLOCK, BLOCK)
        loads.append(pltpu.make_async_copy(v_hbm.at[:, cols], v.at[:, cols], load_sem.at[1 + j]))
    loads.append(pltpu.make_async_copy(c_hbm, c, load_sem.at[5]))
    for j in range(4):
        cols = pl.ds(j * BLOCK, BLOCK)
        loads.append(pltpu.make_async_copy(u_hbm.at[:, cols], u.at[:, cols], load_sem.at[6 + j]))
    for load in loads:
        load.start()

    barrier = pltpu.get_barrier_semaphore()
    for other in others:
        pl.semaphore_signal(barrier, inc=1, device_id=(other, core), device_id_type=MESH)
    pl.semaphore_signal(barrier, inc=1, device_id=twin, device_id_type=MESH)

    sum_a = Sum(0, bits, others, core, acc_a, out_a, got_a, mid_a, full_a, send_a, recv_a)
    sum_b = Sum(1, bits, others, core, acc_b, out_b, got_b, mid_b, full_b, send_b, recv_b)

    def partial(left, right, total, j):
        block = jnp.dot(left[...], right[:, j * BLOCK:(j + 1) * BLOCK], preferred_element_type=F32)
        for side in range(2):
            tiles = block[:, side * 128:(side + 1) * 128].reshape(32, 16, 128)
            where = pl.ds(64 * j + 32 * side, 32)
            total.acc[where] = tiles
            total.out[where] = tiles.astype(BF16)

    def first_sends(total, j):
        for part in range(6):
            end = total.starts[part] + total.sizes[part]
            if 64 * j < end <= 64 * (j + 1):
                total.send(part, 0)

    loads[0].wait()
    for j in range(4):
        loads[1 + j].wait()
        partial(f, v, sum_a, j)
        if j == 0:
            pl.semaphore_wait(barrier, 7)
        first_sends(sum_a, j)

    loads[5].wait()

    @pl.loop(0, COLS // BLOCK)
    def _(i):
        cols = pl.ds(pl.multiple_of(i * BLOCK, BLOCK), BLOCK)
        lift = (c[:, cols].astype(F32) * f[:, cols].astype(F32)).astype(BF16)
        d[:, cols] = lift
        bias_own[:, cols] = jnp.broadcast_to(jnp.sum(lift.astype(F32), axis=0, keepdims=True), (8, BLOCK))

    for j in range(4):
        loads[6 + j].wait()
        partial(d, u, sum_b, j)
        first_sends(sum_b, j)

    def to_twin(source, target, k):
        copy = pltpu.make_async_remote_copy(
            src_ref=source, dst_ref=target, send_sem=twin_send.at[k], recv_sem=twin_recv.at[k],
            device_id=twin, device_id_type=MESH,
        )
        copy.start()
        return copy

    to_twins = [to_twin(bias_own, bias_twin, 0)]
    for k, (source, target) in enumerate(((d, dt), (f, ft))):
        @pl.loop(0, COLS // 128)
        def _(i):
            at = pl.multiple_of(i * 128, 128)
            target[core, pl.ds(at, 128), :] = source[:, pl.ds(at, 128)].T

        to_twins.append(to_twin(target.at[core], target.at[core], 1 + k))

    for stage in range(STAGES):
        sum_a.step(stage)
        sum_b.step(stage)

    to_twins.append(to_twin(full_a.at[pl.ds((1 - core) * 128, 128)], twin_a, 3))
    to_twins.append(to_twin(full_b.at[pl.ds((1 - core) * 128, 128)], twin_b, 4))

    for full, flat, half in ((full_a, codes, half_a), (full_b, dcodes, half_b)):
        for j in range(8):
            flat[:, j * 128:(j + 1) * 128] = full[32 * j:32 * (j + 1)].reshape(ROWS, 128)
        for j in range(4):
            half[core, :, j * 128:(j + 1) * 128] = full[pl.ds(core * 128 + 32 * j, 32)].reshape(ROWS, 128)

    nt = (((1,), (1,)), ((), ()))

    @pl.loop(0, COLS // BLOCK)
    def _(i):
        cols = pl.ds(pl.multiple_of(i * BLOCK, BLOCK), BLOCK)
        lifted = lax.dot_general(codes[...], u[cols, :], nt, preferred_element_type=F32)
        base[:, cols] = c[:, cols].astype(F32) * (lifted + b_ref[:, cols] + 1.0)

    @pl.loop(0, COLS // BLOCK)
    def _(i):
        cols = pl.ds(pl.multiple_of(i * BLOCK, BLOCK), BLOCK)
        back = lax.dot_general(dcodes[...], v[cols, :], nt, preferred_element_type=F32)
        gi[:, cols] = (base[:, cols] + back).astype(BF16)
        pltpu.make_async_copy(gi.at[:, cols], gi_hbm.at[:, cols], store_sem.at[0, i]).start()

    for k, (other, half) in enumerate(((twin_a, half_a), (twin_b, half_b))):
        to_twins[3 + k].wait_recv()
        for j in range(4):
            half[1 - core, :, j * 128:(j + 1) * 128] = other[32 * j:32 * (j + 1)].reshape(ROWS, 128)

    for k, (left, right, result, target) in enumerate(((dt, half_a, gu, gu_hbm), (ft, half_b, gv, gv_hbm))):
        to_twins[1 + k].wait_recv()

        @pl.loop(0, COLS // BLOCK)
        def _(i):
            rows = pl.ds(pl.multiple_of(i * BLOCK, BLOCK), BLOCK)
            value = jnp.dot(left[0, rows, :], right[0], preferred_element_type=F32)
            value += jnp.dot(left[1, rows, :], right[1], preferred_element_type=F32)
            result[rows, :] = value.astype(BF16)
            pltpu.make_async_copy(result.at[rows, :], target.at[rows, :], store_sem.at[1 + k, i]).start()

    to_twins[0].wait_recv()
    gb_ref[...] = bias_own[0:1, :] + bias_twin[0:1, :]

    @pl.loop(0, COLS // BLOCK)
    def _(i):
        cols = pl.ds(pl.multiple_of(i * BLOCK, BLOCK), BLOCK)
        pltpu.make_async_copy(gi.at[:, cols], gi_hbm.at[:, cols], store_sem.at[0, i]).wait()
        pltpu.make_async_copy(gu.at[cols, :], gu_hbm.at[cols, :], store_sem.at[1, i]).wait()
        pltpu.make_async_copy(gv.at[cols, :], gv_hbm.at[cols, :], store_sem.at[2, i]).wait()

    sum_a.finish()
    sum_b.finish()
    for copy in to_twins:
        copy.wait_send()


def shards(features, cotangent, u_rows, v_rows, bias):
    anywhere, vmem = pl.BlockSpec(memory_space=pl.ANY), pl.BlockSpec(memory_space=pltpu.VMEM)
    tiles = (TILES, 16, 128)
    dma = pltpu.SemaphoreType.DMA
    grad_input, grad_u, grad_v, grad_bias = pl.pallas_call(
        kernel,
        out_shape=(
            jax.ShapeDtypeStruct((ROWS, COLS), BF16),
            jax.ShapeDtypeStruct((COLS, RANK // 2), BF16),
            jax.ShapeDtypeStruct((COLS, RANK // 2), BF16),
            jax.ShapeDtypeStruct((1, COLS), F32),
        ),
        in_specs=[anywhere] * 4 + [vmem],
        out_specs=(anywhere, anywhere, anywhere, vmem),
        scratch_shapes=[
            pltpu.VMEM((ROWS, COLS), BF16), pltpu.VMEM((ROWS, COLS), BF16),
            pltpu.VMEM((COLS, RANK), BF16), pltpu.VMEM((COLS, RANK), BF16),
            pltpu.VMEM((ROWS, COLS), BF16),
            pltpu.VMEM(tiles, F32), pltpu.VMEM(tiles, F32),
            pltpu.VMEM(tiles, BF16), pltpu.VMEM(tiles, BF16),
            pltpu.VMEM((272, 16, 128), BF16), pltpu.VMEM((272, 16, 128), BF16),
            pltpu.VMEM((32, 16, 128), BF16), pltpu.VMEM((32, 16, 128), BF16),
            pltpu.VMEM(tiles, BF16), pltpu.VMEM(tiles, BF16),
            pltpu.VMEM((2, COLS, ROWS), BF16), pltpu.VMEM((2, COLS, ROWS), BF16),
            pltpu.VMEM((ROWS, COLS), F32),
            pltpu.VMEM((ROWS, RANK), BF16), pltpu.VMEM((ROWS, RANK), BF16),
            pltpu.VMEM((2, ROWS, RANK // 2), BF16), pltpu.VMEM((2, ROWS, RANK // 2), BF16),
            pltpu.VMEM((128, 16, 128), BF16), pltpu.VMEM((128, 16, 128), BF16),
            pltpu.VMEM((ROWS, COLS), BF16),
            pltpu.VMEM((COLS, RANK // 2), BF16), pltpu.VMEM((COLS, RANK // 2), BF16),
            pltpu.VMEM((8, COLS), F32), pltpu.VMEM((8, COLS), F32),
            dma((10,)), dma((3, COLS // BLOCK)),
            dma((STAGES, 6)), dma((STAGES, 6)), dma((STAGES, 6)), dma((STAGES, 6)),
            dma((5,)), dma((5,)),
        ],
        compiler_params=pltpu.CompilerParams(collective_id=0, has_side_effects=True, vmem_limit_bytes=60 << 20),
    )(features, cotangent, u_rows, v_rows, bias.reshape(1, COLS))
    return grad_input, grad_u, grad_v, grad_bias.reshape(COLS)


def solution(mesh):
    in_specs = (P("batch", "feat"), P("batch", "feat"), P("feat", None), P("feat", None), P("feat"))
    out_specs = (P("batch", "feat"), P("feat", "batch"), P("feat", "batch"), P("feat"))
    return jax.shard_map(shards, mesh=mesh, in_specs=in_specs, out_specs=out_specs, check_vma=False)
```

time: 474 us -> 80.9 us (0.17)
  blocking collectives: 403 us -> 0 us
  Pallas kernels: 0 us -> 72.4 us
  matrix products: 35.2 us -> 0 us
  between operations: 14.1 us -> 0.65 us
  other arithmetic: 9.07 us -> 0 us
  waiting for transfers between devices: 8.85 us -> 0 us
  local copies, waits for them, and re-layouts: 2.53 us -> 7.58 us
    psum x2 -> x0, blocking collectives: 403 us -> none  [the longest x1 400 us: shards(): codes = lax.psum(partial_codes, 'feat').astype(jnp.bfloat16)]
    pallas_call x0 -> x1, Pallas kernels: none -> 72.4 us  [shards(): pl.pallas_call(kernel, out_shape=(jax.ShapeDtypeStruct((ROWS, COLS), BF16...]
    dot_general x6 -> x0, matrix products: 35.2 us -> none  [the longest x1 8.77 us: shards(): lax.dot_general(dlift, codes, (((0,), (0,)), ((), ())), preferred_element...]
    reduce_scatter x2 -> x0, waiting for transfers between devices: 8.82 us -> none  [the longest x1 8.82 us: shards(): lax.psum_scatter(local_u, 'batch', scatter_dimension=1, tiled=True)]
    convert_element_type x2 -> x0, other arithmetic: 6.27 us -> none  [the longest x1 3.77 us: shards(): grad_u = summed_u.astype(jnp.bfloat16)]
    unnamed x13 -> x10, local copies, waits for them, and re-layouts: 2.53 us -> 7.58 us
  transfers between devices with their start and end apart: 2 -> 0, of which waited for: 1 -> 0; matrix products, arithmetic and copies ran while one was open for 5% -> 0% of each run, Pallas kernels for 0% -> 0%
where the time goes in v1:
time: 80.9 us; the launch traced here: 80.7 us
  Pallas kernels  72.4 us (89%)
  local copies, waits for them, and re-layouts  7.58 us (9%)
    pallas_call x1, Pallas kernels, shards(): pl.pallas_call(kernel, out_shape=(jax.ShapeDtypeStruct((ROWS, COLS), BF16...  72.4 us
    unnamed x10, local copies, waits for them, and re-layouts  7.58 us

profile of v1, /device:TPU:0, one launch (start us, length us, event | category | flops | bytes accessed | tf_op | source)
XLA Modules:
  0.0 80.7 jit_solution(13057578175078357779)
XLA Ops:
  0.6 72.4 %shard_map.84 = (bf16[512,2048]{1,0:T(8,128)(2,1)}, bf16[2048,512]{1,0:T(8,128)(2,1)}, bf16[2048,512]{1,0:T(8,128)(2,1)}, f32[1,2048]{1,0:T(1,128)}) custom-call(bf16[512,2048]{1,0:T(8,128)(2,1)} %f_hbm.1, bf16[512,2048]{1,0:T(8,128)(2,1)} %c_hbm.1, bf16[2048,1024]{1,0:T(8,128)(2,1)} %u_hbm.1, bf16[2048,1024]{1,0:T(8,128)(2,1)} %v_hbm.1, f32[1,2048]{1,0:T(1,128)} %bitcast.3), custom_call_target="tpu_custom_call" | custom-call | tf_op jit(solution)/shard_map/pallas_call | solution.py:259
  73.1 0.0 copy-start.1
  73.1 3.3 %copy.13 = bf16[512,2048]{1,0:T(8,128)(2,1)} copy(bf16[512,2048]{1,0:T(8,128)(2,1)} %get-tuple-element.16) | data formatting | bytes 4194304
  76.4 0.0 copy-done.1
  76.4 0.0 copy-start
  76.4 1.3 %copy.14 = bf16[2048,512]{1,0:T(8,128)(2,1)} copy(bf16[2048,512]{1,0:T(8,128)(2,1)S(1)} %copy-done.1) | data formatting | bytes 4194304
  77.7 1.0 %copy-done = bf16[2048,512]{1,0:T(8,128)(2,1)S(1)} copy-done((bf16[2048,512]{1,0:T(8,128)(2,1)S(1)}, bf16[2048,512]{1,0:T(8,128)(2,1)}, u32[]{:S(2)}) %copy-start) | copy-done | bytes 2097176
  78.8 0.0 copy-start.2
  78.8 1.3 %copy.15 = bf16[2048,512]{1,0:T(8,128)(2,1)} copy(bf16[2048,512]{1,0:T(8,128)(2,1)S(1)} %copy-done) | data formatting | bytes 4194304
  80.1 0.0 copy-done.2
  80.1 0.6 copy.16
Async XLA Ops:
  73.1 3.3 %copy-start.1 = (bf16[2048,512]{1,0:T(8,128)(2,1)S(1)}, bf16[2048,512]{1,0:T(8,128)(2,1)}, u32[]{:S(2)}) copy-start(bf16[2048,512]{1,0:T(8,128)(2,1)} %get-tuple-element.17) | copy-start | bytes 6291460
  76.4 2.3 %copy-start = (bf16[2048,512]{1,0:T(8,128)(2,1)S(1)}, bf16[2048,512]{1,0:T(8,128)(2,1)}, u32[]{:S(2)}) copy-start(bf16[2048,512]{1,0:T(8,128)(2,1)} %get-tuple-element.18) | copy-start | bytes 6291460
  78.8 1.3 %copy-start.2 = (f32[1,2048]{1,0:T(1,128)S(1)}, f32[1,2048]{1,0:T(1,128)}, u32[]{:S(2)}) copy-start(f32[1,2048]{1,0:T(1,128)} %get-tuple-element.11) | copy-start | bytes 24580

commit v2 on v1

v2 whole, which is shorter than its diff:
```python
import jax
import jax.numpy as jnp
from jax import lax
from jax.experimental import pallas as pl
from jax.experimental.pallas import tpu as pltpu
from jax.sharding import PartitionSpec as P

MESH = pl.DeviceIdType.MESH
F32, BF16 = jnp.float32, jnp.bfloat16
NT = (((1,), (1,)), ((), ()))
ROWS, COLS, RANK = 512, 2048, 1024
HALF, BLOCK = RANK // 2, 256
BLOCKS = COLS // BLOCK
TILES = 256
STAGES, PARTS = 5, 3
SIZES = ((96, 80, 80), (80, 96, 80))
AXES = ((16, 0), (4, 0), (1, 0), (16, 1), (4, 1), (1, 1))
PAIRS = ((0, 4), (1, 5), (2, 3))


def hypercube(feat):
    bits, steps = [], []
    for stride, kind in AXES:
        place = lax.rem(lax.div(feat, stride), 4)
        if kind == 0:
            bits.append(lax.rem(lax.div(place + 1, 2), 2))
            steps.append((1 - 2 * lax.rem(place, 2)) * stride)
        else:
            bits.append(lax.div(place, 2))
            steps.append((3 - 2 * place) * stride)
    return bits, steps


def squares(feat):
    bits, steps = hypercube(feat)
    result = []
    for high, low in PAIRS:
        quarters, chips = [], []
        for flip in range(4):
            far, near = flip // 2, flip % 2
            quarters.append(2 * (1 - bits[high] if far else bits[high]) + (1 - bits[low] if near else bits[low]))
            chips.append(feat + far * steps[high] + near * steps[low])
        result.append((quarters, chips))
    return result


class Sum:
    def __init__(self, index, places, core, acc, out, got, mid, full, send_sem, recv_sem):
        self.index, self.places, self.core = index, places, core
        self.acc, self.out, self.got, self.mid, self.full = acc, out, got, mid, full
        self.send_sem, self.recv_sem = send_sem, recv_sem
        self.sizes = SIZES[index]
        self.starts = [sum(self.sizes[:part]) for part in range(PARTS)]
        self.copies, self.past = {}, {}
        self.region = dict(enumerate(zip(self.starts, self.sizes)))
        offset, self.offset = 0, {}
        for stage in range(3):
            for part in range(PARTS):
                self.offset[stage, part] = offset
                offset += 3 * (self.sizes[part] >> min(2 * stage + 2, 4))

    def square(self, part, stage):
        return self.places[(part + min(stage, STAGES - 1 - stage) + self.index) % PARTS]

    def slot(self, part, stage, flip, size):
        return pl.ds(self.offset[stage, part] + (flip - 1) * size, size)

    def send(self, part, stage):
        quarters, chips = self.square(part, stage)
        start, size = self.region[part]
        if stage < 2:
            size //= 4
            self.past[stage, part] = start
            self.region[part] = (start + quarters[0] * size, size)
        for flip in (3, 2, 1):
            if stage < 2:
                source = self.out.at[pl.ds(start + quarters[flip] * size, size)]
                target = self.got.at[self.slot(part, stage, flip, size)]
            elif stage == 2:
                source = self.mid.at[pl.ds(self.starts[part] // 16, size)]
                target = self.got.at[self.slot(part, stage, flip, size)]
            else:
                source = target = self.full.at[pl.ds(start, size)]
            copy = pltpu.make_async_remote_copy(
                src_ref=source,
                dst_ref=target,
                send_sem=self.send_sem.at[stage, part, flip - 1],
                recv_sem=self.recv_sem.at[stage, part, flip - 1],
                device_id=(chips[flip], self.core),
                device_id_type=MESH,
            )
            copy.start()
            self.copies[stage, part, flip] = copy

    def receive(self, part, stage):
        for flip in (1, 2, 3):
            self.copies[stage, part, flip].wait_recv()
        start, size = self.region[part]
        if stage > 2:
            self.region[part] = (self.past[STAGES - 1 - stage, part], 4 * size)
            return
        here = pl.ds(start, size)
        value = self.acc[here]
        for flip in (1, 2, 3):
            value += self.got[self.slot(part, stage, flip, size)].astype(F32)
        if stage == 2:
            self.full[here] = value.astype(BF16)
            return
        self.acc[here] = value
        if stage == 0:
            self.out[here] = value.astype(BF16)
        else:
            self.mid[pl.ds(self.starts[part] // 16, size)] = value.astype(BF16)

    def step(self, stage):
        for part in range(PARTS):
            self.receive(part, stage)
            if stage + 1 < STAGES:
                self.send(part, stage + 1)

    def finish(self):
        for copy in self.copies.values():
            copy.wait_send()


def kernel(
    f_hbm, c_hbm, u_hbm, v_hbm, b_ref, gi, gu, ft, half_b, gb_ref,
    f, c, u, v, d, acc_a, acc_b, out_a, out_b, got_a, got_b, mid_a, mid_b, full_a, full_b,
    dt, base, codes, dcodes, half_a, twin_a, twin_b, bias_own, bias_twin,
    load_sem, send_a, recv_a, send_b, recv_b, twin_send, twin_recv,
):
    feat, core = lax.axis_index("feat"), lax.axis_index("batch")
    twin = (feat, 1 - core)
    places = squares(feat)

    loads = [pltpu.make_async_copy(f_hbm, f, load_sem.at[0])]
    for j in range(4):
        cols = pl.ds(j * BLOCK, BLOCK)
        loads.append(pltpu.make_async_copy(v_hbm.at[:, cols], v.at[:, cols], load_sem.at[1 + j]))
    loads.append(pltpu.make_async_copy(c_hbm, c, load_sem.at[5]))
    for j in range(4):
        cols = pl.ds(j * BLOCK, BLOCK)
        loads.append(pltpu.make_async_copy(u_hbm.at[:, cols], u.at[:, cols], load_sem.at[6 + j]))
    for load in loads:
        load.start()

    barrier = pltpu.get_barrier_semaphore()
    for _, chips in places:
        for flip in (1, 2, 3):
            pl.semaphore_signal(barrier, inc=1, device_id=(chips[flip], core), device_id_type=MESH)
    pl.semaphore_signal(barrier, inc=1, device_id=twin, device_id_type=MESH)

    sum_a = Sum(0, places, core, acc_a, out_a, got_a, mid_a, full_a, send_a, recv_a)
    sum_b = Sum(1, places, core, acc_b, out_b, got_b, mid_b, full_b, send_b, recv_b)

    def partial(left, right, total, j):
        block = jnp.dot(left[...], right[:, j * BLOCK:(j + 1) * BLOCK], preferred_element_type=F32)
        for side in range(2):
            tiles = block[:, side * 128:(side + 1) * 128].reshape(32, 16, 128)
            where = pl.ds(64 * j + 32 * side, 32)
            total.acc[where] = tiles
            total.out[where] = tiles.astype(BF16)

    def first_sends(total, j):
        for part in range(PARTS):
            end = total.starts[part] + total.sizes[part]
            if 64 * j < end <= 64 * (j + 1):
                total.send(part, 0)

    loads[0].wait()
    for j in range(4):
        loads[1 + j].wait()
        partial(f, v, sum_a, j)
        if j == 1:
            pl.semaphore_wait(barrier, 10)
        first_sends(sum_a, j)

    loads[5].wait()

    @pl.loop(0, BLOCKS)
    def _(i):
        cols = pl.ds(pl.multiple_of(i * BLOCK, BLOCK), BLOCK)
        lift = (c[:, cols].astype(F32) * f[:, cols].astype(F32)).astype(BF16)
        d[:, cols] = lift
        bias_own[:, cols] = jnp.broadcast_to(jnp.sum(lift.astype(F32), axis=0, keepdims=True), (8, BLOCK))

    for j in range(4):
        loads[6 + j].wait()
        partial(d, u, sum_b, j)
        first_sends(sum_b, j)

    def to_twin(source, target, k):
        copy = pltpu.make_async_remote_copy(
            src_ref=source, dst_ref=target, send_sem=twin_send.at[k], recv_sem=twin_recv.at[k],
            device_id=twin, device_id_type=MESH,
        )
        copy.start()
        return copy

    to_twins = [to_twin(bias_own, bias_twin, 0)]
    for k, (source, target) in enumerate(((d, dt), (f, ft))):

        @pl.loop(0, COLS // 128)
        def _(i):
            at = pl.multiple_of(i * 128, 128)
            target[core, pl.ds(at, 128), :] = source[:, pl.ds(at, 128)].T

        to_twins.append(to_twin(target.at[core], target.at[core], 1 + k))

    def flatten(full, flat, half):
        for j in range(8):
            flat[:, j * 128:(j + 1) * 128] = full[32 * j:32 * (j + 1)].reshape(ROWS, 128)
        for j in range(4):
            half[core, :, j * 128:(j + 1) * 128] = full[pl.ds(core * 128 + 32 * j, 32)].reshape(ROWS, 128)

    def other_half(other, half):
        for j in range(4):
            half[1 - core, :, j * 128:(j + 1) * 128] = other[32 * j:32 * (j + 1)].reshape(ROWS, 128)

    sum_a.step(0)
    sum_a.step(1)
    sum_b.step(0)
    sum_a.step(2)
    sum_b.step(1)
    sum_a.step(3)
    sum_b.step(2)
    sum_a.step(4)
    to_twins.append(to_twin(full_a.at[pl.ds((1 - core) * 128, 128)], twin_a, 3))
    sum_b.step(3)
    flatten(full_a, codes, half_a)

    @pl.loop(0, BLOCKS)
    def _(i):
        cols = pl.ds(pl.multiple_of(i * BLOCK, BLOCK), BLOCK)
        lifted = lax.dot_general(codes[...], u[cols, :], NT, preferred_element_type=F32)
        base[:, cols] = c[:, cols].astype(F32) * (lifted + b_ref[:, cols] + 1.0)

    to_twins[3].wait_recv()
    other_half(twin_a, half_a)
    to_twins[1].wait_recv()

    @pl.loop(0, BLOCKS)
    def _(i):
        rows = pl.ds(pl.multiple_of(i * BLOCK, BLOCK), BLOCK)
        value = jnp.dot(dt[0, rows, :], half_a[0], preferred_element_type=F32)
        value += jnp.dot(dt[1, rows, :], half_a[1], preferred_element_type=F32)
        gu[rows, :] = value.astype(BF16)

    to_twins[0].wait_recv()
    gb_ref[...] = bias_own[0:1, :] + bias_twin[0:1, :]

    sum_b.step(4)
    to_twins.append(to_twin(full_b.at[pl.ds((1 - core) * 128, 128)], twin_b, 4))
    flatten(full_b, dcodes, half_b)

    @pl.loop(0, BLOCKS)
    def _(i):
        cols = pl.ds(pl.multiple_of(i * BLOCK, BLOCK), BLOCK)
        back = lax.dot_general(dcodes[...], v[cols, :], NT, preferred_element_type=F32)
        gi[:, cols] = (base[:, cols] + back).astype(BF16)

    to_twins[4].wait_recv()
    other_half(twin_b, half_b)
    to_twins[2].wait_recv()
    sum_a.finish()
    sum_b.finish()
    for copy in to_twins:
        copy.wait_send()


def last_kernel(gi, gu, ft, half_b, gb, gi_hbm, gu_hbm, gv_hbm, gb_hbm, gv, sem):
    copies = [
        pltpu.make_async_copy(gi, gi_hbm, sem.at[0]),
        pltpu.make_async_copy(gu, gu_hbm, sem.at[1]),
        pltpu.make_async_copy(gb, gb_hbm, sem.at[2]),
    ]
    for copy in copies:
        copy.start()
    for i in range(BLOCKS):
        rows = pl.ds(i * BLOCK, BLOCK)
        value = jnp.dot(ft[0, rows, :], half_b[0], preferred_element_type=F32)
        value += jnp.dot(ft[1, rows, :], half_b[1], preferred_element_type=F32)
        gv[rows, :] = value.astype(BF16)
        copies.append(pltpu.make_async_copy(gv.at[rows, :], gv_hbm.at[rows, :], sem.at[3 + i]))
        copies[-1].start()
    for copy in copies:
        copy.wait()


def shards(features, cotangent, u_rows, v_rows, bias):
    anywhere, vmem = pl.BlockSpec(memory_space=pl.ANY), pl.BlockSpec(memory_space=pltpu.VMEM)
    tiles = (TILES, 16, 128)
    dma = pltpu.SemaphoreType.DMA
    inner = pl.pallas_call(
        kernel,
        out_shape=(
            pltpu.VMEM((ROWS, COLS), BF16),
            pltpu.VMEM((COLS, HALF), BF16),
            pltpu.VMEM((2, COLS, ROWS), BF16),
            pltpu.VMEM((2, ROWS, HALF), BF16),
            pltpu.VMEM((1, COLS), F32),
        ),
        in_specs=[anywhere] * 4 + [vmem],
        out_specs=(vmem,) * 5,
        scratch_shapes=[
            pltpu.VMEM((ROWS, COLS), BF16), pltpu.VMEM((ROWS, COLS), BF16),
            pltpu.VMEM((COLS, RANK), BF16), pltpu.VMEM((COLS, RANK), BF16),
            pltpu.VMEM((ROWS, COLS), BF16),
            pltpu.VMEM(tiles, F32), pltpu.VMEM(tiles, F32),
            pltpu.VMEM(tiles, BF16), pltpu.VMEM(tiles, BF16),
            pltpu.VMEM((288, 16, 128), BF16), pltpu.VMEM((288, 16, 128), BF16),
            pltpu.VMEM((16, 16, 128), BF16), pltpu.VMEM((16, 16, 128), BF16),
            pltpu.VMEM(tiles, BF16), pltpu.VMEM(tiles, BF16),
            pltpu.VMEM((2, COLS, ROWS), BF16),
            pltpu.VMEM((ROWS, COLS), F32),
            pltpu.VMEM((ROWS, RANK), BF16), pltpu.VMEM((ROWS, RANK), BF16),
            pltpu.VMEM((2, ROWS, HALF), BF16),
            pltpu.VMEM((128, 16, 128), BF16), pltpu.VMEM((128, 16, 128), BF16),
            pltpu.VMEM((8, COLS), F32), pltpu.VMEM((8, COLS), F32),
            dma((10,)),
            dma((STAGES, PARTS, 3)), dma((STAGES, PARTS, 3)), dma((STAGES, PARTS, 3)), dma((STAGES, PARTS, 3)),
            dma((5,)), dma((5,)),
        ],
        compiler_params=pltpu.CompilerParams(collective_id=0, has_side_effects=True, vmem_limit_bytes=46 << 20),
    )(features, cotangent, u_rows, v_rows, bias.reshape(1, COLS))
    grad_input, grad_u, grad_v, grad_bias = pl.pallas_call(
        last_kernel,
        out_shape=(
            jax.ShapeDtypeStruct((ROWS, COLS), BF16),
            jax.ShapeDtypeStruct((COLS, HALF), BF16),
            jax.ShapeDtypeStruct((COLS, HALF), BF16),
            jax.ShapeDtypeStruct((1, COLS), F32),
        ),
        in_specs=[vmem] * 5,
        out_specs=(anywhere,) * 4,
        scratch_shapes=[pltpu.VMEM((COLS, HALF), BF16), dma((3 + BLOCKS,))],
        compiler_params=pltpu.CompilerParams(vmem_limit_bytes=16 << 20),
    )(*inner)
    return grad_input, grad_u, grad_v, grad_bias.reshape(COLS)


def solution(mesh):
    in_specs = (P("batch", "feat"), P("batch", "feat"), P("feat", None), P("feat", None), P("feat"))
    out_specs = (P("batch", "feat"), P("feat", "batch"), P("feat", "batch"), P("feat"))
    return jax.shard_map(shards, mesh=mesh, in_specs=in_specs, out_specs=out_specs, check_vma=False)
```

time: 80.9 us -> 57.9 us (0.72)
  Pallas kernels: 72.4 us -> 57.1 us
  local copies, waits for them, and re-layouts: 7.58 us -> 0 us
    pallas_call x1 -> x2, Pallas kernels: 72.4 us -> 57.1 us  [the longest x1 54 us: shards(): pl.pallas_call(kernel, out_shape=(pltpu.VMEM((ROWS, COLS), BF16), pltpu.V...]
    unnamed x10 -> x0, local copies, waits for them, and re-layouts: 7.58 us -> none
where the time goes in v2:
time: 57.9 us; the launch traced here: 57.8 us
  Pallas kernels  57.1 us (99%)
  between operations  0.64 us (1%)
    pallas_call x1, Pallas kernels, shards(): pl.pallas_call(kernel, out_shape=(pltpu.VMEM((ROWS, COLS), BF16), pltpu.V...  54 us
    pallas_call x1, Pallas kernels, shards(): pl.pallas_call(last_kernel, out_shape=(jax.ShapeDtypeStruct((ROWS, COLS),...  3.14 us

profile of v2, /device:TPU:0, one launch (start us, length us, event | category | flops | bytes accessed | tf_op | source)
XLA Modules:
  0.0 57.8 jit_solution(11116255680702444373)
XLA Ops:
  0.6 54.0 %shard_map.84 = (bf16[512,2048]{1,0:T(8,128)(2,1)S(1)}, bf16[2048,512]{1,0:T(8,128)(2,1)S(1)}, bf16[2,2048,512]{2,1,0:T(8,128)(2,1)S(1)}, bf16[2,512,512]{2,1,0:T(8,128)(2,1)S(1)}, f32[1,2048]{1,0:T(1,128)S(1)}) custom-call(bf16[512,2048]{1,0:T(8,128)(2,1)} %f_hbm.1, bf16[512,2048]{1,0:T(8,128)(2,1)} %c_hbm.1, bf16[2048,1024]{1,0:T(8,128)(2,1)} %u_hbm.1, ...), custom_call_target="tpu_custom_call" | custom-call | tf_op jit(solution)/shard_map/pallas_call | solution.py:294
  54.6 3.1 %shard_map.85 = (bf16[512,2048]{1,0:T(8,128)(2,1)}, bf16[2048,512]{1,0:T(8,128)(2,1)}, bf16[2048,512]{1,0:T(8,128)(2,1)}, f32[1,2048]{1,0:T(1,128)}) custom-call(bf16[512,2048]{1,0:T(8,128)(2,1)S(1)} %get-tuple-element.13.gi, bf16[2048,512]{1,0:T(8,128)(2,1)S(1)} %get-tuple-element.14.gu, bf16[2,2048,512]{2,1,0:T(8,128)(2,1)S(1)} %get-tuple-element.15.ft, ...), custom_call_target="tpu_custom_call" | custom-call | tf_op jit(solution)/shard_map/pallas_call | solution.py:326

commit v3 on v2

--- a/solution.py
+++ b/solution.py
@@ -133,16 +133,24 @@
     twin = (feat, 1 - core)
     places = squares(feat)
 
-    loads = [pltpu.make_async_copy(f_hbm, f, load_sem.at[0])]
+    loads = {}
+
+    def load(name, source, target):
+        loads[name] = pltpu.make_async_copy(source, target, load_sem.at[len(loads)])
+        loads[name].start()
+
+    def load_block(name, source, target, j):
+        cols = pl.ds(j * BLOCK, BLOCK)
+        load((name, j), source.at[:, cols], target.at[:, cols])
+
+    load("f", f_hbm, f)
+    load_block("v", v_hbm, v, 0)
+    load_block("v", v_hbm, v, 1)
+    load("c", c_hbm, c)
+    load_block("v", v_hbm, v, 2)
+    load_block("v", v_hbm, v, 3)
     for j in range(4):
-        cols = pl.ds(j * BLOCK, BLOCK)
-        loads.append(pltpu.make_async_copy(v_hbm.at[:, cols], v.at[:, cols], load_sem.at[1 + j]))
-    loads.append(pltpu.make_async_copy(c_hbm, c, load_sem.at[5]))
-    for j in range(4):
-        cols = pl.ds(j * BLOCK, BLOCK)
-        loads.append(pltpu.make_async_copy(u_hbm.at[:, cols], u.at[:, cols], load_sem.at[6 + j]))
-    for load in loads:
-        load.start()
+        load_block("u", u_hbm, u, j)
 
     barrier = pltpu.get_barrier_semaphore()
     for _, chips in places:
@@ -167,25 +175,24 @@
             if 64 * j < end <= 64 * (j + 1):
                 total.send(part, 0)
 
-    loads[0].wait()
+    def lift(lower, upper):
+        for i in range(lower, upper, BLOCK):
+            cols = slice(i, i + BLOCK)
+            d[:, cols] = (c[:, cols].astype(F32) * f[:, cols].astype(F32)).astype(BF16)
+
+    loads["f"].wait()
     for j in range(4):
-        loads[1 + j].wait()
+        loads["v", j].wait()
+        if j == 2:
+            loads["c"].wait()
         partial(f, v, sum_a, j)
+        if j >= 2:
+            lift((j - 2) * COLS // 2, (j - 1) * COLS // 2)
         if j == 1:
             pl.semaphore_wait(barrier, 10)
         first_sends(sum_a, j)
-
-    loads[5].wait()
-
-    @pl.loop(0, BLOCKS)
-    def _(i):
-        cols = pl.ds(pl.multiple_of(i * BLOCK, BLOCK), BLOCK)
-        lift = (c[:, cols].astype(F32) * f[:, cols].astype(F32)).astype(BF16)
-        d[:, cols] = lift
-        bias_own[:, cols] = jnp.broadcast_to(jnp.sum(lift.astype(F32), axis=0, keepdims=True), (8, BLOCK))
-
     for j in range(4):
-        loads[6 + j].wait()
+        loads["u", j].wait()
         partial(d, u, sum_b, j)
         first_sends(sum_b, j)
 
@@ -197,15 +204,15 @@
         copy.start()
         return copy
 
-    to_twins = [to_twin(bias_own, bias_twin, 0)]
+    to_twins = {}
     for k, (source, target) in enumerate(((d, dt), (f, ft))):
-
-        @pl.loop(0, COLS // 128)
-        def _(i):
-            at = pl.multiple_of(i * 128, 128)
-            target[core, pl.ds(at, 128), :] = source[:, pl.ds(at, 128)].T
-
-        to_twins.append(to_twin(target.at[core], target.at[core], 1 + k))
+        for i in range(0, COLS, BLOCK):
+            target[core, i:i + BLOCK, :] = source[:, i:i + BLOCK].T
+        to_twins[k] = to_twin(target.at[core], target.at[core], k)
+    for i in range(0, COLS, BLOCK):
+        total = jnp.sum(d[:, i:i + BLOCK].astype(F32), axis=0, keepdims=True)
+        bias_own[:, i:i + BLOCK] = jnp.broadcast_to(total, (8, BLOCK))
+    to_twins[2] = to_twin(bias_own, bias_twin, 2)
 
     def flatten(full, flat, half):
         for j in range(8):
@@ -217,54 +224,39 @@
         for j in range(4):
             half[1 - core, :, j * 128:(j + 1) * 128] = other[32 * j:32 * (j + 1)].reshape(ROWS, 128)
 
-    sum_a.step(0)
-    sum_a.step(1)
-    sum_b.step(0)
-    sum_a.step(2)
-    sum_b.step(1)
-    sum_a.step(3)
-    sum_b.step(2)
-    sum_a.step(4)
-    to_twins.append(to_twin(full_a.at[pl.ds((1 - core) * 128, 128)], twin_a, 3))
-    sum_b.step(3)
+    for total, stage in (
+        (sum_a, 0), (sum_a, 1), (sum_b, 0), (sum_a, 2), (sum_b, 1), (sum_a, 3), (sum_b, 2), (sum_b, 3), (sum_a, 4),
+    ):
+        total.step(stage)
+    to_twins[3] = to_twin(full_a.at[pl.ds((1 - core) * 128, 128)], twin_a, 3)
     flatten(full_a, codes, half_a)
-
-    @pl.loop(0, BLOCKS)
-    def _(i):
-        cols = pl.ds(pl.multiple_of(i * BLOCK, BLOCK), BLOCK)
+    for i in range(0, COLS, BLOCK):
+        cols = slice(i, i + BLOCK)
         lifted = lax.dot_general(codes[...], u[cols, :], NT, preferred_element_type=F32)
         base[:, cols] = c[:, cols].astype(F32) * (lifted + b_ref[:, cols] + 1.0)
-
     to_twins[3].wait_recv()
     other_half(twin_a, half_a)
-    to_twins[1].wait_recv()
-
-    @pl.loop(0, BLOCKS)
-    def _(i):
-        rows = pl.ds(pl.multiple_of(i * BLOCK, BLOCK), BLOCK)
-        value = jnp.dot(dt[0, rows, :], half_a[0], preferred_element_type=F32)
-        value += jnp.dot(dt[1, rows, :], half_a[1], preferred_element_type=F32)
-        gu[rows, :] = value.astype(BF16)
-
     to_twins[0].wait_recv()
+    for i in range(0, COLS, BLOCK):
+        value = jnp.dot(dt[0, i:i + BLOCK, :], half_a[0], preferred_element_type=F32)
+        value += jnp.dot(dt[1, i:i + BLOCK, :], half_a[1], preferred_element_type=F32)
+        gu[i:i + BLOCK, :] = value.astype(BF16)
+    to_twins[2].wait_recv()
     gb_ref[...] = bias_own[0:1, :] + bias_twin[0:1, :]
 
     sum_b.step(4)
-    to_twins.append(to_twin(full_b.at[pl.ds((1 - core) * 128, 128)], twin_b, 4))
+    to_twins[4] = to_twin(full_b.at[pl.ds((1 - core) * 128, 128)], twin_b, 4)
     flatten(full_b, dcodes, half_b)
-
-    @pl.loop(0, BLOCKS)
-    def _(i):
-        cols = pl.ds(pl.multiple_of(i * BLOCK, BLOCK), BLOCK)
+    for i in range(0, COLS, BLOCK):
+        cols = slice(i, i + BLOCK)
         back = lax.dot_general(dcodes[...], v[cols, :], NT, preferred_element_type=F32)
         gi[:, cols] = (base[:, cols] + back).astype(BF16)
-
     to_twins[4].wait_recv()
     other_half(twin_b, half_b)
-    to_twins[2].wait_recv()
+    to_twins[1].wait_recv()
     sum_a.finish()
     sum_b.finish()
-    for copy in to_twins:
+    for copy in to_twins.values():
         copy.wait_send()
 
 

time: 57.9 us -> 53 us (0.915); the launches traced: 57.8 us -> 52.2 us
  Pallas kernels: 57.1 us -> 51.4 us
    pallas_call x1, Pallas kernels: 54 us -> 48.2 us  [shards(): pl.pallas_call(kernel, out_shape=(pltpu.VMEM((ROWS, COLS), BF16), pltpu.V...]
where the time goes in v3:
time: 53 us; the launch traced here: 52.2 us
  Pallas kernels  51.4 us (97%)
  between operations  0.8 us (2%)
    pallas_call x1, Pallas kernels, shards(): pl.pallas_call(kernel, out_shape=(pltpu.VMEM((ROWS, COLS), BF16), pltpu.V...  48.2 us
    pallas_call x1, Pallas kernels, shards(): pl.pallas_call(last_kernel, out_shape=(jax.ShapeDtypeStruct((ROWS, COLS),...  3.14 us

profile of v3, /device:TPU:0, one launch (start us, length us, event | category | flops | bytes accessed | tf_op | source)
XLA Modules:
  0.0 52.2 jit_solution(15959582682914612719)
XLA Ops:
  0.6 48.2 %shard_map.84 = (bf16[512,2048]{1,0:T(8,128)(2,1)S(1)}, bf16[2048,512]{1,0:T(8,128)(2,1)S(1)}, bf16[2,2048,512]{2,1,0:T(8,128)(2,1)S(1)}, bf16[2,512,512]{2,1,0:T(8,128)(2,1)S(1)}, f32[1,2048]{1,0:T(1,128)S(1)}) custom-call(bf16[512,2048]{1,0:T(8,128)(2,1)} %f_hbm.1, bf16[512,2048]{1,0:T(8,128)(2,1)} %c_hbm.1, bf16[2048,1024]{1,0:T(8,128)(2,1)} %u_hbm.1, ...), custom_call_target="tpu_custom_call" | custom-call | tf_op jit(solution)/shard_map/pallas_call | solution.py:286
  48.9 3.1 %shard_map.85 = (bf16[512,2048]{1,0:T(8,128)(2,1)}, bf16[2048,512]{1,0:T(8,128)(2,1)}, bf16[2048,512]{1,0:T(8,128)(2,1)}, f32[1,2048]{1,0:T(1,128)}) custom-call(bf16[512,2048]{1,0:T(8,128)(2,1)S(1)} %get-tuple-element.13.gi, bf16[2048,512]{1,0:T(8,128)(2,1)S(1)} %get-tuple-element.14.gu, bf16[2,2048,512]{2,1,0:T(8,128)(2,1)S(1)} %get-tuple-element.15.ft, ...), custom_call_target="tpu_custom_call" | custom-call | tf_op jit(solution)/shard_map/pallas_call | solution.py:318

commit v4 on v3

--- a/solution.py
+++ b/solution.py
@@ -15,7 +15,7 @@
 STAGES, PARTS = 5, 3
 SIZES = ((96, 80, 80), (80, 96, 80))
 AXES = ((16, 0), (4, 0), (1, 0), (16, 1), (4, 1), (1, 1))
-PAIRS = ((0, 4), (1, 5), (2, 3))
+PAIRS = ((0, 3), (1, 4), (2, 5))
 
 
 def hypercube(feat):
@@ -39,7 +39,12 @@
         for flip in range(4):
             far, near = flip // 2, flip % 2
             quarters.append(2 * (1 - bits[high] if far else bits[high]) + (1 - bits[low] if near else bits[low]))
-            chips.append(feat + far * steps[high] + near * steps[low])
+            if flip == 3:
+                stride = AXES[high][0]
+                place = lax.rem(lax.div(feat, stride), 4)
+                chips.append(feat + (lax.rem(place + 2, 4) - place) * stride)
+            else:
+                chips.append(feat + far * steps[high] + near * steps[low])
         result.append((quarters, chips))
     return result
 
@@ -72,7 +77,7 @@
             size //= 4
             self.past[stage, part] = start
             self.region[part] = (start + quarters[0] * size, size)
-        for flip in (3, 2, 1):
+        for flip in (3, 1, 2):
             if stage < 2:
                 source = self.out.at[pl.ds(start + quarters[flip] * size, size)]
                 target = self.got.at[self.slot(part, stage, flip, size)]
@@ -118,9 +123,10 @@
             if stage + 1 < STAGES:
                 self.send(part, stage + 1)
 
-    def finish(self):
-        for copy in self.copies.values():
-            copy.wait_send()
+    def finish(self, stages):
+        for (stage, _, _), copy in self.copies.items():
+            if stage in stages:
+                copy.wait_send()
 
 
 def kernel(
@@ -146,11 +152,6 @@
     load("f", f_hbm, f)
     load_block("v", v_hbm, v, 0)
     load_block("v", v_hbm, v, 1)
-    load("c", c_hbm, c)
-    load_block("v", v_hbm, v, 2)
-    load_block("v", v_hbm, v, 3)
-    for j in range(4):
-        load_block("u", u_hbm, u, j)
 
     barrier = pltpu.get_barrier_semaphore()
     for _, chips in places:
@@ -175,22 +176,22 @@
             if 64 * j < end <= 64 * (j + 1):
                 total.send(part, 0)
 
-    def lift(lower, upper):
-        for i in range(lower, upper, BLOCK):
-            cols = slice(i, i + BLOCK)
-            d[:, cols] = (c[:, cols].astype(F32) * f[:, cols].astype(F32)).astype(BF16)
-
     loads["f"].wait()
+    load_block("v", v_hbm, v, 2)
+    load_block("v", v_hbm, v, 3)
+    load("c", c_hbm, c)
     for j in range(4):
         loads["v", j].wait()
-        if j == 2:
-            loads["c"].wait()
+        if j == 0:
+            for k in range(4):
+                load_block("u", u_hbm, u, k)
         partial(f, v, sum_a, j)
-        if j >= 2:
-            lift((j - 2) * COLS // 2, (j - 1) * COLS // 2)
         if j == 1:
             pl.semaphore_wait(barrier, 10)
         first_sends(sum_a, j)
+    loads["c"].wait()
+    for i in range(0, COLS, BLOCK):
+        d[:, i:i + BLOCK] = c[:, i:i + BLOCK] * f[:, i:i + BLOCK]
     for j in range(4):
         loads["u", j].wait()
         partial(d, u, sum_b, j)
@@ -244,6 +245,10 @@
     to_twins[2].wait_recv()
     gb_ref[...] = bias_own[0:1, :] + bias_twin[0:1, :]
 
+    sum_a.finish(range(STAGES))
+    sum_b.finish(range(4))
+    for k in range(4):
+        to_twins[k].wait_send()
     sum_b.step(4)
     to_twins[4] = to_twin(full_b.at[pl.ds((1 - core) * 128, 128)], twin_b, 4)
     flatten(full_b, dcodes, half_b)
@@ -254,10 +259,8 @@
     to_twins[4].wait_recv()
     other_half(twin_b, half_b)
     to_twins[1].wait_recv()
-    sum_a.finish()
-    sum_b.finish()
-    for copy in to_twins.values():
-        copy.wait_send()
+    sum_b.finish((4,))
+    to_twins[4].wait_send()
 
 
 def last_kernel(gi, gu, ft, half_b, gb, gi_hbm, gu_hbm, gv_hbm, gb_hbm, gv, sem):

time: 53 us -> 52 us (0.981)
  no operation moved by 1% of the time
where the time goes in v4:
time: 52 us; the launch traced here: 51.7 us
  Pallas kernels  50.9 us (98%)
  between operations  0.8 us (2%)
    pallas_call x1, Pallas kernels, shards(): pl.pallas_call(kernel, out_shape=(pltpu.VMEM((ROWS, COLS), BF16), pltpu.V...  47.7 us
    pallas_call x1, Pallas kernels, shards(): pl.pallas_call(last_kernel, out_shape=(jax.ShapeDtypeStruct((ROWS, COLS),...  3.14 us

profile of v4, /device:TPU:0, one launch (start us, length us, event | category | flops | bytes accessed | tf_op | source)
XLA Modules:
  0.0 51.7 jit_solution(5122407847320800865)
XLA Ops:
  0.6 47.7 %shard_map.84 = (bf16[512,2048]{1,0:T(8,128)(2,1)S(1)}, bf16[2048,512]{1,0:T(8,128)(2,1)S(1)}, bf16[2,2048,512]{2,1,0:T(8,128)(2,1)S(1)}, bf16[2,512,512]{2,1,0:T(8,128)(2,1)S(1)}, f32[1,2048]{1,0:T(1,128)S(1)}) custom-call(bf16[512,2048]{1,0:T(8,128)(2,1)} %f_hbm.1, bf16[512,2048]{1,0:T(8,128)(2,1)} %c_hbm.1, bf16[2048,1024]{1,0:T(8,128)(2,1)} %u_hbm.1, ...), custom_call_target="tpu_custom_call" | custom-call | tf_op jit(solution)/shard_map/pallas_call | solution.py:289
  48.4 3.1 %shard_map.85 = (bf16[512,2048]{1,0:T(8,128)(2,1)}, bf16[2048,512]{1,0:T(8,128)(2,1)}, bf16[2048,512]{1,0:T(8,128)(2,1)}, f32[1,2048]{1,0:T(1,128)}) custom-call(bf16[512,2048]{1,0:T(8,128)(2,1)S(1)} %get-tuple-element.13.gi, bf16[2048,512]{1,0:T(8,128)(2,1)S(1)} %get-tuple-element.14.gu, bf16[2,2048,512]{2,1,0:T(8,128)(2,1)S(1)} %get-tuple-element.15.ft, ...), custom_call_target="tpu_custom_call" | custom-call | tf_op jit(solution)/shard_map/pallas_call | solution.py:321

commit v5 on v4

--- a/solution.py
+++ b/solution.py
@@ -130,8 +130,8 @@
 
 
 def kernel(
-    f_hbm, c_hbm, u_hbm, v_hbm, b_ref, gi, gu, ft, half_b, gb_ref,
-    f, c, u, v, d, acc_a, acc_b, out_a, out_b, got_a, got_b, mid_a, mid_b, full_a, full_b,
+    f_hbm, c_hbm, u_hbm, v_hbm, b_hbm, gi, gu, ft, half_b, gb_ref,
+    f, c, u, v, b, d, acc_a, acc_b, out_a, out_b, got_a, got_b, mid_a, mid_b, full_a, full_b,
     dt, base, codes, dcodes, half_a, twin_a, twin_b, bias_own, bias_twin,
     load_sem, send_a, recv_a, send_b, recv_b, twin_send, twin_recv,
 ):
@@ -185,6 +185,7 @@
         if j == 0:
             for k in range(4):
                 load_block("u", u_hbm, u, k)
+            load("b", b_hbm, b)
         partial(f, v, sum_a, j)
         if j == 1:
             pl.semaphore_wait(barrier, 10)
@@ -231,10 +232,11 @@
         total.step(stage)
     to_twins[3] = to_twin(full_a.at[pl.ds((1 - core) * 128, 128)], twin_a, 3)
     flatten(full_a, codes, half_a)
+    loads["b"].wait()
     for i in range(0, COLS, BLOCK):
         cols = slice(i, i + BLOCK)
         lifted = lax.dot_general(codes[...], u[cols, :], NT, preferred_element_type=F32)
-        base[:, cols] = c[:, cols].astype(F32) * (lifted + b_ref[:, cols] + 1.0)
+        base[:, cols] = c[:, cols].astype(F32) * (lifted + b[:, cols] + 1.0)
     to_twins[3].wait_recv()
     other_half(twin_a, half_a)
     to_twins[0].wait_recv()
@@ -295,11 +297,11 @@
             pltpu.VMEM((2, ROWS, HALF), BF16),
             pltpu.VMEM((1, COLS), F32),
         ),
-        in_specs=[anywhere] * 4 + [vmem],
+        in_specs=[anywhere] * 5,
         out_specs=(vmem,) * 5,
         scratch_shapes=[
             pltpu.VMEM((ROWS, COLS), BF16), pltpu.VMEM((ROWS, COLS), BF16),
-            pltpu.VMEM((COLS, RANK), BF16), pltpu.VMEM((COLS, RANK), BF16),
+            pltpu.VMEM((COLS, RANK), BF16), pltpu.VMEM((COLS, RANK), BF16), pltpu.VMEM((1, COLS), F32),
             pltpu.VMEM((ROWS, COLS), BF16),
             pltpu.VMEM(tiles, F32), pltpu.VMEM(tiles, F32),
             pltpu.VMEM(tiles, BF16), pltpu.VMEM(tiles, BF16),
@@ -312,7 +314,7 @@
             pltpu.VMEM((2, ROWS, HALF), BF16),
             pltpu.VMEM((128, 16, 128), BF16), pltpu.VMEM((128, 16, 128), BF16),
             pltpu.VMEM((8, COLS), F32), pltpu.VMEM((8, COLS), F32),
-            dma((10,)),
+            dma((11,)),
             dma((STAGES, PARTS, 3)), dma((STAGES, PARTS, 3)), dma((STAGES, PARTS, 3)), dma((STAGES, PARTS, 3)),
             dma((5,)), dma((5,)),
         ],

time: 52 us -> 51.3 us (0.987)
  Pallas kernels: 50.9 us -> 50.2 us
    pallas_call x1, Pallas kernels: 47.7 us -> 47.1 us  [shards(): pl.pallas_call(kernel, out_shape=(pltpu.VMEM((ROWS, COLS), BF16), pltpu.V...]
where the time goes in v5:
time: 51.3 us; the launch traced here: 51 us
  Pallas kernels  50.2 us (98%)
  between operations  0.8 us (2%)
    pallas_call x1, Pallas kernels, shards(): pl.pallas_call(kernel, out_shape=(pltpu.VMEM((ROWS, COLS), BF16), pltpu.V...  47.1 us
    pallas_call x1, Pallas kernels, shards(): pl.pallas_call(last_kernel, out_shape=(jax.ShapeDtypeStruct((ROWS, COLS),...  3.14 us

profile of v5, /device:TPU:0, one launch (start us, length us, event | category | flops | bytes accessed | tf_op | source)
XLA Modules:
  0.0 51.0 jit_solution(8237525677148175906)
XLA Ops:
  0.6 47.1 %shard_map.84 = (bf16[512,2048]{1,0:T(8,128)(2,1)S(1)}, bf16[2048,512]{1,0:T(8,128)(2,1)S(1)}, bf16[2,2048,512]{2,1,0:T(8,128)(2,1)S(1)}, bf16[2,512,512]{2,1,0:T(8,128)(2,1)S(1)}, f32[1,2048]{1,0:T(1,128)S(1)}) custom-call(bf16[512,2048]{1,0:T(8,128)(2,1)} %f_hbm.1, bf16[512,2048]{1,0:T(8,128)(2,1)} %c_hbm.1, bf16[2048,1024]{1,0:T(8,128)(2,1)} %u_hbm.1, ...), custom_call_target="tpu_custom_call" | custom-call | tf_op jit(solution)/shard_map/pallas_call | solution.py:291
  47.7 3.1 %shard_map.85 = (bf16[512,2048]{1,0:T(8,128)(2,1)}, bf16[2048,512]{1,0:T(8,128)(2,1)}, bf16[2048,512]{1,0:T(8,128)(2,1)}, f32[1,2048]{1,0:T(1,128)}) custom-call(bf16[512,2048]{1,0:T(8,128)(2,1)S(1)} %get-tuple-element.13.gi, bf16[2048,512]{1,0:T(8,128)(2,1)S(1)} %get-tuple-element.14.gu, bf16[2,2048,512]{2,1,0:T(8,128)(2,1)S(1)} %get-tuple-element.15.ft, ...), custom_call_target="tpu_custom_call" | custom-call | tf_op jit(solution)/shard_map/pallas_call | solution.py:323

commit v6 on v5

--- a/solution.py
+++ b/solution.py
@@ -13,7 +13,7 @@
 BLOCKS = COLS // BLOCK
 TILES = 256
 STAGES, PARTS = 5, 3
-SIZES = ((96, 80, 80), (80, 96, 80))
+SIZES = ((96, 80, 80), (96, 80, 80))
 AXES = ((16, 0), (4, 0), (1, 0), (16, 1), (4, 1), (1, 1))
 PAIRS = ((0, 3), (1, 4), (2, 5))
 
@@ -216,9 +216,11 @@
         bias_own[:, i:i + BLOCK] = jnp.broadcast_to(total, (8, BLOCK))
     to_twins[2] = to_twin(bias_own, bias_twin, 2)
 
-    def flatten(full, flat, half):
+    def flatten(full, flat):
         for j in range(8):
             flat[:, j * 128:(j + 1) * 128] = full[32 * j:32 * (j + 1)].reshape(ROWS, 128)
+
+    def own_half(full, half):
         for j in range(4):
             half[core, :, j * 128:(j + 1) * 128] = full[pl.ds(core * 128 + 32 * j, 32)].reshape(ROWS, 128)
 
@@ -231,13 +233,14 @@
     ):
         total.step(stage)
     to_twins[3] = to_twin(full_a.at[pl.ds((1 - core) * 128, 128)], twin_a, 3)
-    flatten(full_a, codes, half_a)
+    flatten(full_a, codes)
     loads["b"].wait()
     for i in range(0, COLS, BLOCK):
         cols = slice(i, i + BLOCK)
         lifted = lax.dot_general(codes[...], u[cols, :], NT, preferred_element_type=F32)
         base[:, cols] = c[:, cols].astype(F32) * (lifted + b[:, cols] + 1.0)
     to_twins[3].wait_recv()
+    own_half(full_a, half_a)
     other_half(twin_a, half_a)
     to_twins[0].wait_recv()
     for i in range(0, COLS, BLOCK):
@@ -253,11 +256,12 @@
         to_twins[k].wait_send()
     sum_b.step(4)
     to_twins[4] = to_twin(full_b.at[pl.ds((1 - core) * 128, 128)], twin_b, 4)
-    flatten(full_b, dcodes, half_b)
+    flatten(full_b, dcodes)
     for i in range(0, COLS, BLOCK):
         cols = slice(i, i + BLOCK)
         back = lax.dot_general(dcodes[...], v[cols, :], NT, preferred_element_type=F32)
         gi[:, cols] = (base[:, cols] + back).astype(BF16)
+    own_half(full_b, half_b)
     to_twins[4].wait_recv()
     other_half(twin_b, half_b)
     to_twins[1].wait_recv()

time: 51.3 us -> 51.2 us (level)
  no operation moved by 1% of the time
where the time goes in v6:
time: 51.2 us; the launch traced here: 50.9 us
  Pallas kernels  50 us (98%)
  between operations  0.8 us (2%)
    pallas_call x1, Pallas kernels, shards(): pl.pallas_call(kernel, out_shape=(pltpu.VMEM((ROWS, COLS), BF16), pltpu.V...  46.9 us
    pallas_call x1, Pallas kernels, shards(): pl.pallas_call(last_kernel, out_shape=(jax.ShapeDtypeStruct((ROWS, COLS),...  3.14 us

profile of v6, /device:TPU:0, one launch (start us, length us, event | category | flops | bytes accessed | tf_op | source)
XLA Modules:
  0.0 50.9 jit_solution(16158518121170091746)
XLA Ops:
  0.6 46.9 %shard_map.84 = (bf16[512,2048]{1,0:T(8,128)(2,1)S(1)}, bf16[2048,512]{1,0:T(8,128)(2,1)S(1)}, bf16[2,2048,512]{2,1,0:T(8,128)(2,1)S(1)}, bf16[2,512,512]{2,1,0:T(8,128)(2,1)S(1)}, f32[1,2048]{1,0:T(1,128)S(1)}) custom-call(bf16[512,2048]{1,0:T(8,128)(2,1)} %f_hbm.1, bf16[512,2048]{1,0:T(8,128)(2,1)} %c_hbm.1, bf16[2048,1024]{1,0:T(8,128)(2,1)} %u_hbm.1, ...), custom_call_target="tpu_custom_call" | custom-call | tf_op jit(solution)/shard_map/pallas_call | solution.py:295
  47.6 3.1 %shard_map.85 = (bf16[512,2048]{1,0:T(8,128)(2,1)}, bf16[2048,512]{1,0:T(8,128)(2,1)}, bf16[2048,512]{1,0:T(8,128)(2,1)}, f32[1,2048]{1,0:T(1,128)}) custom-call(bf16[512,2048]{1,0:T(8,128)(2,1)S(1)} %get-tuple-element.13.gi, bf16[2048,512]{1,0:T(8,128)(2,1)S(1)} %get-tuple-element.14.gu, bf16[2,2048,512]{2,1,0:T(8,128)(2,1)S(1)} %get-tuple-element.15.ft, ...), custom_call_target="tpu_custom_call" | custom-call | tf_op jit(solution)/shard_map/pallas_call | solution.py:327
